TPU v7x, 32 devices: a whole 2x2x4 slice. The times are simulated.
32 devices in a mesh: frame: 4 (over y, x), vox: 8 (over z, core).
Axes of the slice: x: 2, y: 2, z: 4, core: 2. Of those that a mesh axis runs over, the one named last changes fastest.
Arguments:
- volume: float32 [4, 256, 32, 128], P('frame', 'vox'), may hold values from -60 to 60
Outputs:
- factor: float32 [256, 256], replicated
All inputs are finite; a program needn't handle non-finite values.
Results may differ from a plain program's by a relative error of at most 0.0001.
Values sent between devices are 32-bit elements; how exact they have to be, the bound alone decides.
A program may use at most 64 MiB of HBM per device.

v0:
```python
import jax
import jax.numpy as jnp
from jax import lax
from jax.sharding import PartitionSpec as P


def block_gram(block, scale):
    rows_z = block.shape[1]
    column_block = jnp.moveaxis(block, 1, 0).reshape(rows_z, -1)
    return jnp.dot(
        column_block,
        column_block.T,
        precision=lax.Precision.HIGHEST,
        preferred_element_type=jnp.float32,
    ) / jnp.float32(scale)


def per_device(volume):
    column_total = float(
        volume.shape[0] * lax.axis_size("frame") * volume.shape[2] * volume.shape[3]
    )
    regrouped = lax.all_to_all(volume, "vox", split_axis=2, concat_axis=1, tiled=True)
    all_frames = lax.all_gather(regrouped, "frame", axis=0, tiled=True)
    local_gram = block_gram(all_frames, column_total)
    gram_all = lax.psum(local_gram, "vox")
    factor = jnp.linalg.cholesky(gram_all)
    return factor


def solution(mesh):
    return jax.shard_map(
        per_device,
        mesh=mesh,
        in_specs=(P("frame", "vox", None, None),),
        out_specs=P(),
        check_vma=False,
    )
```

profile of v0, /device:TPU:0, one launch (start us, length us, event | category | flops | bytes accessed | tf_op | source)
XLA Modules:
  0.0 170.0 jit_solution(12618962765040331475)
XLA Ops:
  6.5 0.0 all-gather.2.cloned.1.call-start
  6.5 1.3 copy.5
  7.9 21.5 %all_to_all.18 = f32[1,32,32,128]{3,1,0,2:T(8,128)S(1)} all-to-all(f32[1,32,32,128]{3,1,0,2:T(8,128)S(1)} %copy.5), channel_id=1, replica_groups=mesh['frame'=4,'vox'=8] {'vox'}, dimensions={2} | all-to-all | bytes 1048576 | tf_op jit(solution)/shard_map/all_to_all | solution.py:22
  29.4 0.8 copy.6
  30.2 0.0 all-gather.2.cloned.1.call-update
  30.2 0.0 all-reduce.3.cloned.1.call-start
  30.3 34.3 %all-gather.2.cloned.1.call-done = f32[4,256,4,128]{3,1,2,0:T(8,128)} async-done(((f32[1,256,4,128]{3,1,2,0:T(8,128)}), f32[4,256,4,128]{3,1,2,0:T(8,128)}) %all-gather.2.cloned.1.call-update) | async-done | bytes 2097168 | tf_op jit(solution)/shard_map/all_gather | solution.py:23
  64.6 4.8 %fusion.5 = f32[256,256]{0,1:T(8,128)} fusion(f32[4,256,4,128]{3,1,2,0:T(8,128)} %all-gather.2.cloned.1.call-done), kind=kOutput, calls=%fused_computation.3 | convolution fusion | flops 1610678272 | bytes 2359296 | tf_op jit(solution)/shard_map/dot_general | solution.py:10
  69.4 0.0 all-reduce.3.cloned.1.call-update
  69.4 55.0 %all-reduce.3.cloned.1.call-done = f32[256,256]{0,1:T(8,128)} async-done(((f32[256,256]{0,1:T(8,128)}), f32[256,256]{0,1:T(8,128)}) %all-reduce.3.cloned.1.call-update) | async-done | bytes 262160 | tf_op jit(solution)/shard_map/psum | solution.py:25
  124.4 1.1 copy.8
  125.5 1.0 fusion.8
  126.5 11.7 %cholesky.50 = f32[128,128]{1,0:T(8,128)S(1)} custom-call(f32[128,128]{1,0:T(8,128)S(1)} %cholesky.118), custom_call_target="Cholesky" | custom-call | tf_op jit(solution)/shard_map/jit(cholesky)/cholesky | solution.py:26
  138.3 9.8 %custom-call.11 = f32[1,128,128]{1,2,0:T(8,128)S(1)} custom-call(f32[1,128,128]{2,1,0:T(8,128)S(1)} %get-tuple-element.8), custom_call_target="InvertDiagBlocksLowerTriangular" | custom-call | tf_op jit(solution)/shard_map/jit(cholesky)/cholesky | solution.py:26
  148.1 0.2 constant_dynamic-update-slice_fusion.1
  148.3 0.3 convolution_subtract_fusion
  148.6 11.7 %cholesky.105 = f32[128,128]{1,0:T(8,128)S(1)} custom-call(f32[128,128]{1,0:T(8,128)S(1)} %convolution_subtract_fusion), custom_call_target="Cholesky" | custom-call | tf_op jit(solution)/shard_map/jit(cholesky)/cholesky | solution.py:26
  160.3 0.7 compare_reduce_fusion
  162.4 0.7 select_select_fusion
  (4 shorter events, 0.1 us)
Async XLA Ops:
  6.5 58.1 %all-gather.2.cloned.1.call-start = ((), (), s32[]{:S(2)}) async-start(), calls=%async_computation.1 | async-start | bytes 2621440 | tf_op jit(solution)/shard_map/all_gather | solution.py:23
  30.2 94.2 %all-reduce.3.cloned.1.call-start = ((), (), s32[]{:S(2)}) async-start(), calls=%async_computation.2 | async-start | bytes 524288 | tf_op jit(solution)/shard_map/psum | solution.py:25
Sparse Core Ops, SparseCore 0:
  30.4 34.2 all-gather.1
  69.5 54.8 all-reduce.2
where the time goes:
time: 170 us
  waiting for transfers between devices  89.4 us (53%)
  other arithmetic  35.7 us (21%)
  blocking collectives  21.5 us (13%)
  between operations  14.8 us (9%)
  matrix products  5.25 us (3%)
  local copies, waits for them, and re-layouts  3.29 us (2%)
    psum x1, waiting for transfers between devices, per_device(): gram_all = lax.psum(local_gram, 'vox')  55 us
    all_gather x1, waiting for transfers between devices, per_device(): all_frames = lax.all_gather(regrouped, 'frame', axis=0, tiled=True)  34.3 us
    another operation x6, other arithmetic, per_device(): factor = jnp.linalg.cholesky(gram_all)  34 us
    all_to_all x1, blocking collectives, per_device(): lax.all_to_all(volume, 'vox', split_axis=2, concat_axis=1, tiled=True)  21.5 us
    dot_general x1, matrix products, block_gram(): jnp.dot(column_block, column_block.T, precision=lax.Precision.HIGHEST, pr...  4.78 us
  transfers between devices with their start and end apart: 2, of which 2 were waited for; matrix products, arithmetic and copies ran while one was open for 0% of the time, Pallas kernels for 0%

commit v1 on v0

v1 whole, which is shorter than its diff:
```python
import functools

import jax
import jax.numpy as jnp
from jax import lax
from jax.experimental import pallas as pl
from jax.experimental.pallas import tpu as pltpu
from jax.sharding import PartitionSpec as P

MESH = pl.DeviceIdType.MESH
CORES = 2
EXACT = lax.Precision.HIGHEST


def gram_kernel(
    frames, voxes, rows_z, rows_x, columns,
    vol_ref, out_ref,
    send, recv, part, plane, line, total,
    a_send, a_recv, b_send, b_recv, c_send, c_recv, d_send, d_recv,
):
    f = lax.axis_index("frame")
    v = lax.axis_index("vox")
    chip, core = v // CORES, v % CORES
    chips = voxes // CORES
    own = f * CORES + core
    members = frames * CORES
    xd = rows_x // voxes
    slot = rows_z * xd
    half = rows_z * voxes // 2
    share = 2 * half // members

    def plane_peer(k):
        q = lax.rem(own + k, members)
        return q, (q // CORES, chip * CORES + q % CORES)

    def line_peer(k):
        c = lax.rem(chip + k, chips)
        return c, (f, c * CORES + core)

    barrier = pltpu.get_barrier_semaphore()
    for k in range(1, voxes):
        pl.semaphore_signal(
            barrier, inc=1, device_id=(f, lax.rem(v + k, voxes)), device_id_type=MESH
        )
    for k in range(1, members):
        pl.semaphore_signal(
            barrier, inc=1, device_id=plane_peer(k)[1], device_id_type=MESH
        )

    for p in range(voxes):
        for x in range(xd):
            send[p, pl.ds(x, rows_z, stride=xd), :] = vol_ref[
                pl.ds(p * xd + x, rows_z, stride=rows_x), :
            ]

    pl.semaphore_wait(barrier, voxes - 1 + members - 1)

    mine = pl.ds(pl.multiple_of(v * slot, slot), slot)
    copies = []
    for k in sorted(range(1, voxes), key=lambda k: abs(k - voxes // 2)):
        p = lax.rem(v + k, voxes)
        copy = pltpu.make_async_remote_copy(
            src_ref=send.at[p],
            dst_ref=recv.at[mine],
            send_sem=a_send.at[k],
            recv_sem=a_recv.at[k],
            device_id=(f, p),
            device_id_type=MESH,
        )
        copy.start()
        copies.append(copy)
    recv[mine, :] = send[v]
    for copy in copies:
        copy.wait()

    block = jnp.concatenate(
        [recv[pl.ds(x, 2 * half, stride=xd), :] for x in range(xd)], axis=1
    )
    top, low = block[:half], block[half:]

    def dot(a, b):
        return lax.dot_general(
            a, b, (((1,), (1,)), ((), ())),
            precision=EXACT, preferred_element_type=jnp.float32,
        )

    i = lax.broadcasted_iota(jnp.int32, (half, half), 0)
    j = lax.broadcasted_iota(jnp.int32, (half, half), 1)
    g22 = dot(low, low)
    diag = jnp.sum(jnp.where(i == j, g22, 0.0), axis=0, keepdims=True)
    diag = jnp.broadcast_to(diag, (8, half))
    packed = [dot(low, top), jnp.where(i >= j, dot(top, top), g22)]
    for q in range(members):
        row = q * share
        part[q, :share, :] = packed[row // half][row % half:row % half + share]
        part[q, share:, :] = diag

    copies = []
    for k in range(1, members):
        q, device = plane_peer(k)
        copy = pltpu.make_async_remote_copy(
            src_ref=part.at[q],
            dst_ref=plane.at[own],
            send_sem=b_send.at[k],
            recv_sem=b_recv.at[k],
            device_id=device,
            device_id_type=MESH,
        )
        copy.start()
        copies.append(copy)
    plane[own] = part[own]
    for copy in copies:
        copy.wait()

    line[chip] = jnp.sum(plane[...], axis=0)
    copies = []
    for k in range(1, chips):
        c, device = line_peer(k)
        copy = pltpu.make_async_remote_copy(
            src_ref=line.at[chip],
            dst_ref=line.at[chip],
            send_sem=c_send.at[k],
            recv_sem=c_recv.at[k],
            device_id=device,
            device_id_type=MESH,
        )
        copy.start()
        copies.append(copy)
    for copy in copies:
        copy.wait()

    total[own] = jnp.sum(line[...], axis=0) / jnp.float32(columns)
    copies = []
    for k in range(1, members):
        q, device = plane_peer(k)
        copy = pltpu.make_async_remote_copy(
            src_ref=total.at[own],
            dst_ref=total.at[own],
            send_sem=d_send.at[k],
            recv_sem=d_recv.at[k],
            device_id=device,
            device_id_type=MESH,
        )
        copy.start()
        copies.append(copy)
    for copy in copies:
        copy.wait()
    out_ref[...] = total[...]


def summed_gram(volume):
    frames, voxes = lax.axis_size("frame"), lax.axis_size("vox")
    rows_z, rows_x, lanes = volume.shape[1:]
    columns = float(volume.shape[0] * frames * rows_x * lanes)
    xd = rows_x // voxes
    members = frames * CORES
    full = rows_z * voxes
    half = full // 2
    share = full // members
    packed = (members, share + 8, half)
    dma = pltpu.SemaphoreType.DMA
    vmem = pl.BlockSpec(memory_space=pltpu.VMEM)
    return pl.pallas_call(
        functools.partial(gram_kernel, frames, voxes, rows_z, rows_x, columns),
        out_shape=jax.ShapeDtypeStruct(packed, jnp.float32),
        in_specs=[vmem],
        out_specs=vmem,
        scratch_shapes=[
            pltpu.VMEM((voxes, rows_z * xd, lanes), jnp.float32),
            pltpu.VMEM((full * xd, lanes), jnp.float32),
            pltpu.VMEM(packed, jnp.float32),
            pltpu.VMEM(packed, jnp.float32),
            pltpu.VMEM((voxes // CORES, share + 8, half), jnp.float32),
            pltpu.VMEM(packed, jnp.float32),
            dma((voxes,)), dma((voxes,)),
            dma((members,)), dma((members,)),
            dma((voxes // CORES,)), dma((voxes // CORES,)),
            dma((members,)), dma((members,)),
        ],
        compiler_params=pltpu.CompilerParams(
            collective_id=0, has_side_effects=True, vmem_limit_bytes=24 * 1024 * 1024
        ),
        name="summed_gram",
    )(volume.reshape(rows_z * rows_x, lanes))


def per_device(volume):
    packed = summed_gram(volume)
    members, rows, half = packed.shape
    share = rows - 8
    main = packed[:, :share].reshape(2 * half, half)
    diag = packed[0, share]
    g21, mixed = main[:half], main[half:]
    i = lax.broadcasted_iota(jnp.int32, (half, half), 0)
    j = lax.broadcasted_iota(jnp.int32, (half, half), 1)
    g22 = jnp.where(i == j, diag[None, :], mixed.T)
    gram = jnp.concatenate(
        [
            jnp.concatenate([mixed, g21.T], axis=1),
            jnp.concatenate([g21, g22], axis=1),
        ],
        axis=0,
    )
    return lax.linalg.cholesky(gram, symmetrize_input=False)


def solution(mesh):
    return jax.shard_map(
        per_device,
        mesh=mesh,
        in_specs=(P("frame", "vox", None, None),),
        out_specs=P(),
        check_vma=False,
    )
```

time: 170 us -> 68 us (0.40)
  waiting for transfers between devices: 89.4 us -> 0 us
  Pallas kernels: 0 us -> 29.8 us
  blocking collectives: 21.5 us -> 0 us
  between operations: 14.8 us -> 1.43 us
  matrix products: 5.25 us -> 0.57 us
  local copies, waits for them, and re-layouts: 3.29 us -> 1.26 us
    psum x1 -> x0, waiting for transfers between devices: 55 us -> none  [per_device(): gram_all = lax.psum(local_gram, 'vox')]
    all_gather x1 -> x0, waiting for transfers between devices: 34.3 us -> none  [per_device(): all_frames = lax.all_gather(regrouped, 'frame', axis=0, tiled=True)]
    pallas_call x0 -> x1, Pallas kernels: none -> 29.8 us  [summed_gram(): pl.pallas_call(functools.partial(gram_kernel, frames, voxes, rows_z, rows...]
    all_to_all x1 -> x0, blocking collectives: 21.5 us -> none  [per_device(): lax.all_to_all(volume, 'vox', split_axis=2, concat_axis=1, tiled=True)]
    dot_general x1 -> x0, matrix products: 4.78 us -> none  [block_gram(): jnp.dot(column_block, column_block.T, precision=lax.Precision.HIGHEST, pr...]
  transfers between devices with their start and end apart: 2 -> 0, of which waited for: 2 -> 0; matrix products, arithmetic and copies ran while one was open for 0% -> 0% of each run, Pallas kernels for 0% -> 0%
where the time goes in v1:
time: 68 us; the launch traced here: 67.8 us
  other arithmetic  34.8 us (51%)
  Pallas kernels  29.8 us (44%)
  between operations  1.43 us (2%)
  local copies, waits for them, and re-layouts  1.26 us (2%)
    another operation x6, other arithmetic, per_device(): return lax.linalg.cholesky(gram, symmetrize_input=False)  34 us
    pallas_call x1, Pallas kernels, summed_gram(): pl.pallas_call(functools.partial(gram_kernel, frames, voxes, rows_z, rows...  29.8 us

profile of v1, /device:TPU:0, one launch (start us, length us, event | category | flops | bytes accessed | tf_op | source)
XLA Modules:
  0.0 67.8 jit_solution(14627451749408520989)
XLA Ops:
  0.0 0.0 copy-start
  0.0 1.0 %copy-done = f32[1,32,32,128]{3,2,1,0:T(8,128)S(1)} copy-done((f32[1,32,32,128]{3,2,1,0:T(8,128)S(1)}, f32[1,32,32,128]{3,2,1,0:T(8,128)}, u32[]{:S(2)}) %copy-start) | copy-done | bytes 524312
  1.0 29.8 %summed_gram.1 = f32[8,40,128]{2,1,0:T(8,128)S(1)} custom-call(f32[1024,128]{1,0:T(8,128)S(1)} %bitcast.19), custom_call_target="tpu_custom_call" | custom-call | tf_op jit(solution)/shard_map/summed_gram/pallas_call | solution.py:163
  30.9 11.7 %cholesky.50 = f32[128,128]{1,0:T(8,128)S(1)} custom-call(f32[128,128]{1,0:T(8,128)S(1)} %bitcast.21), custom_call_target="Cholesky" | custom-call | tf_op jit(solution)/shard_map/cholesky | solution.py:204
  42.6 0.1 copy.5
  42.8 9.8 %custom-call.8 = f32[1,128,128]{1,2,0:T(8,128)S(1)} custom-call(f32[1,128,128]{2,1,0:T(8,128)S(1)} %get-tuple-element.10), custom_call_target="InvertDiagBlocksLowerTriangular" | custom-call | tf_op jit(solution)/shard_map/cholesky | solution.py:204
  52.6 0.3 fusion
  52.9 0.3 convolution_subtract_fusion
  53.2 0.1 copy.6
  53.3 11.7 %cholesky.104 = f32[128,128]{1,0:T(8,128)S(1)} custom-call(f32[128,128]{1,0:T(8,128)S(1)} %convolution_subtract_fusion), custom_call_target="Cholesky" | custom-call | tf_op jit(solution)/shard_map/cholesky | solution.py:204
  65.1 0.7 %compare_reduce_fusion = (pred[]{:T(512)}, pred[]{:T(512)}) fusion(f32[128]{0:T(128)S(1)} %get-tuple-element.7, f32[128]{0:T(128)S(1)} %get-tuple-element.9), kind=kLoop, calls=%fused_computation.12 | loop fusion | flops 510 | bytes 1026 | tf_op jit(solution)/shard_map/cholesky | solution.py:204
  67.1 0.7 %select_select_fusion = f32[256,256]{1,0:T(8,128)} fusion(f32[256,256]{1,0:T(8,128)S(1)} %get-tuple-element.8, pred[]{:T(512)S(6)} %cholesky.109), kind=kLoop, calls=%fused_computation.1 | loop fusion | flops 196608 | bytes 524289 | tf_op jit(solution)/shard_map/select_n | solution.py:204
  (6 shorter events, 0.1 us)
Async XLA Ops:
  0.0 1.0 %copy-start = (f32[1,32,32,128]{3,2,1,0:T(8,128)S(1)}, f32[1,32,32,128]{3,2,1,0:T(8,128)}, u32[]{:S(2)}) copy-start(f32[1,32,32,128]{3,2,1,0:T(8,128)} %param.1) | copy-start | bytes 1572868

commit v2 on v1

--- a/solution.py
+++ b/solution.py
@@ -10,6 +10,7 @@
 MESH = pl.DeviceIdType.MESH
 CORES = 2
 EXACT = lax.Precision.HIGHEST
+ROWS, LANES = 8, 128
 
 
 def gram_kernel(
@@ -184,24 +185,111 @@
     )(volume.reshape(rows_z * rows_x, lanes))
 
 
+def reciprocal(d):
+    r = pl.reciprocal(d, approx=True)
+    return r * (2.0 - d * r)
+
+
+def inverse_root(d):
+    r = lax.rsqrt(d)
+    return r * (1.5 - 0.5 * d * r * r)
+
+
+def splat_lane(rows, lane):
+    return jnp.broadcast_to(rows[:, lane:lane + 1], (ROWS, LANES))
+
+
+def splat_row(rows, i):
+    return jnp.broadcast_to(rows[i:i + 1], rows.shape)
+
+
+def factor_rows(work, upper, row0):
+    height, width = work.shape
+    panel = work[:ROWS, :]
+    for k in range(0, height, ROWS):
+        columns = [splat_lane(panel[:, :LANES], k + j) for j in range(ROWS)]
+        s = {
+            (i, j): splat_row(columns[j], i) for j in range(ROWS) for i in range(j, ROWS)
+        }
+        rows = [splat_row(panel, i) for i in range(ROWS)]
+        wide = lambda t: jnp.concatenate([t] * (width // LANES), axis=1)
+        inv, low = [], {}
+        for m in range(ROWS):
+            inv.append(reciprocal(s[m, m]))
+            for i in range(m + 1, ROWS):
+                low[i, m] = s[i, m] * inv[m]
+                for j in range(m + 1, i + 1):
+                    s[i, j] = s[i, j] - low[i, m] * s[j, m]
+            for i in range(m + 1, ROWS):
+                rows[i] = rows[i] - wide(low[i, m]) * rows[m]
+        for i in range(ROWS):
+            row = rows[i] * wide(inverse_root(s[i, i]))
+            upper[row0 + k + i:row0 + k + i + 1, :] = row[:1]
+        if k + ROWS == height:
+            break
+        solved = [None] * ROWS
+        for i in reversed(range(ROWS)):
+            solved[i] = rows[i] * wide(inv[i])
+            for m in reversed(range(i + 1, ROWS)):
+                solved[i] = solved[i] - wide(low[m, i]) * solved[m]
+        for g in range(k + ROWS, height, ROWS):
+            group = work[g:g + ROWS, :]
+            terms = [
+                wide(splat_lane(group[:, :LANES], k + j)) * solved[j] for j in range(ROWS)
+            ]
+            while len(terms) > 1:
+                terms = [a + b for a, b in zip(terms[::2], terms[1::2])]
+            group = group - terms[0]
+            if g == k + ROWS:
+                panel = group
+            else:
+                work[g:g + ROWS, :] = group
+
+
+def factor_kernel(packed_ref, out_ref, work1, work2, upper1, upper2):
+    members, rows, half = packed_ref.shape
+    share = rows - ROWS
+    main = [packed_ref[q, :share, :] for q in range(members)]
+    g21 = jnp.concatenate(main[:members // 2], axis=0)
+    mixed = jnp.concatenate(main[members // 2:], axis=0)
+    i = lax.broadcasted_iota(jnp.int32, (half, half), 0)
+    j = lax.broadcasted_iota(jnp.int32, (half, half), 1)
+    flipped = mixed.T
+    work1[:, :half] = jnp.where(i >= j, mixed, flipped)
+    work1[:, half:] = g21.T
+    factor_rows(work1, upper1, 0)
+    right = upper1[:, half:]
+    g22 = jnp.where(i < j, mixed, flipped)
+    g22 = jnp.where(i == j, packed_ref[0, share:share + 1, :], g22)
+    work2[...] = g22 - lax.dot_general(
+        right, right, (((0,), (0,)), ((), ())),
+        precision=EXACT, preferred_element_type=jnp.float32,
+    )
+    factor_rows(work2, upper2, 0)
+    out_ref[:half, :half] = jnp.where(i >= j, upper1[:, :half].T, 0.0)
+    out_ref[:half, half:] = jnp.zeros((half, half), jnp.float32)
+    out_ref[half:, :half] = right.T
+    out_ref[half:, half:] = jnp.where(i >= j, upper2[...].T, 0.0)
+
+
 def per_device(volume):
     packed = summed_gram(volume)
-    members, rows, half = packed.shape
-    share = rows - 8
-    main = packed[:, :share].reshape(2 * half, half)
-    diag = packed[0, share]
-    g21, mixed = main[:half], main[half:]
-    i = lax.broadcasted_iota(jnp.int32, (half, half), 0)
-    j = lax.broadcasted_iota(jnp.int32, (half, half), 1)
-    g22 = jnp.where(i == j, diag[None, :], mixed.T)
-    gram = jnp.concatenate(
-        [
-            jnp.concatenate([mixed, g21.T], axis=1),
-            jnp.concatenate([g21, g22], axis=1),
+    half = packed.shape[2]
+    vmem = pl.BlockSpec(memory_space=pltpu.VMEM)
+    return pl.pallas_call(
+        factor_kernel,
+        out_shape=jax.ShapeDtypeStruct((2 * half, 2 * half), jnp.float32),
+        in_specs=[vmem],
+        out_specs=vmem,
+        scratch_shapes=[
+            pltpu.VMEM((half, 2 * half), jnp.float32),
+            pltpu.VMEM((half, half), jnp.float32),
+            pltpu.VMEM((half, 2 * half), jnp.float32),
+            pltpu.VMEM((half, half), jnp.float32),
         ],
-        axis=0,
-    )
-    return lax.linalg.cholesky(gram, symmetrize_input=False)
+        compiler_params=pltpu.CompilerParams(vmem_limit_bytes=16 * 1024 * 1024),
+        name="factor",
+    )(packed)
 
 
 def solution(mesh):

time: 68 us -> 43.9 us (0.65)
  other arithmetic: 34.8 us -> 0 us
  Pallas kernels: 29.8 us -> 42.7 us
  between operations: 1.43 us -> 0.01 us
    another operation x6 -> x0, other arithmetic: 34 us -> none  [per_device(): return lax.linalg.cholesky(gram, symmetrize_input=False)]
    pallas_call x0 -> x1, Pallas kernels: none -> 12.9 us  [per_device(): pl.pallas_call(factor_kernel, out_shape=jax.ShapeDtypeStruct((2 * half, 2...]
    select_n x1 -> x0, other arithmetic: 0.73 us -> none  [per_device(): return lax.linalg.cholesky(gram, symmetrize_input=False)]
where the time goes in v2:
time: 43.9 us; the launch traced here: 43.7 us
  Pallas kernels  42.7 us (97%)
  local copies, waits for them, and re-layouts  1.04 us (2%)
    pallas_call x1, Pallas kernels, summed_gram(): pl.pallas_call(functools.partial(gram_kernel, frames, voxes, rows_z, rows...  29.8 us
    pallas_call x1, Pallas kernels, per_device(): pl.pallas_call(factor_kernel, out_shape=jax.ShapeDtypeStruct((2 * half, 2...  12.9 us
    unnamed x2, local copies, waits for them, and re-layouts  1.04 us

profile of v2, /device:TPU:0, one launch (start us, length us, event | category | flops | bytes accessed | tf_op | source)
XLA Modules:
  0.0 43.7 jit_solution(9109285474131566319)
XLA Ops:
  0.0 0.0 copy-start
  0.0 1.0 %copy-done = f32[1,32,32,128]{3,2,1,0:T(8,128)S(1)} copy-done((f32[1,32,32,128]{3,2,1,0:T(8,128)S(1)}, f32[1,32,32,128]{3,2,1,0:T(8,128)}, u32[]{:S(2)}) %copy-start) | copy-done | bytes 524312
  1.0 29.8 %summed_gram.1.packed_ref = f32[8,40,128]{2,1,0:T(8,128)S(1)} custom-call(f32[1024,128]{1,0:T(8,128)S(1)} %bitcast.1), custom_call_target="tpu_custom_call" | custom-call | tf_op jit(solution)/shard_map/summed_gram/pallas_call | solution.py:164
  30.9 12.9 %factor.1 = f32[256,256]{1,0:T(8,128)} custom-call(f32[8,40,128]{2,1,0:T(8,128)S(1)} %summed_gram.1.packed_ref), custom_call_target="tpu_custom_call" | custom-call | tf_op jit(solution)/shard_map/factor/pallas_call | solution.py:279
Async XLA Ops:
  0.0 1.0 %copy-start = (f32[1,32,32,128]{3,2,1,0:T(8,128)S(1)}, f32[1,32,32,128]{3,2,1,0:T(8,128)}, u32[]{:S(2)}) copy-start(f32[1,32,32,128]{3,2,1,0:T(8,128)} %param.1) | copy-start | bytes 1572868

commit v3 on v2

--- a/solution.py
+++ b/solution.py
@@ -15,9 +15,9 @@
 
 def gram_kernel(
     frames, voxes, rows_z, rows_x, columns,
-    vol_ref, out_ref,
-    send, recv, part, plane, line, total,
-    a_send, a_recv, b_send, b_recv, c_send, c_recv, d_send, d_recv,
+    vol_hbm, out_ref,
+    vol_ref, send, recv, part, plane, line, total,
+    a_send, a_recv, b_send, b_recv, c_send, c_recv, d_send, d_recv, load_sem,
 ):
     f = lax.axis_index("frame")
     v = lax.axis_index("vox")
@@ -38,6 +38,9 @@
         c = lax.rem(chip + k, chips)
         return c, (f, c * CORES + core)
 
+    load = pltpu.make_async_copy(vol_hbm, vol_ref, load_sem)
+    load.start()
+
     barrier = pltpu.get_barrier_semaphore()
     for k in range(1, voxes):
         pl.semaphore_signal(
@@ -48,6 +51,7 @@
             barrier, inc=1, device_id=plane_peer(k)[1], device_id_type=MESH
         )
 
+    load.wait()
     for p in range(voxes):
         for x in range(xd):
             send[p, pl.ds(x, rows_z, stride=xd), :] = vol_ref[
@@ -89,7 +93,6 @@
     j = lax.broadcasted_iota(jnp.int32, (half, half), 1)
     g22 = dot(low, low)
     diag = jnp.sum(jnp.where(i == j, g22, 0.0), axis=0, keepdims=True)
-    diag = jnp.broadcast_to(diag, (8, half))
     packed = [dot(low, top), jnp.where(i >= j, dot(top, top), g22)]
     for q in range(members):
         row = q * share
@@ -158,25 +161,27 @@
     full = rows_z * voxes
     half = full // 2
     share = full // members
-    packed = (members, share + 8, half)
+    packed = (members, share + 1, half)
     dma = pltpu.SemaphoreType.DMA
     vmem = pl.BlockSpec(memory_space=pltpu.VMEM)
     return pl.pallas_call(
         functools.partial(gram_kernel, frames, voxes, rows_z, rows_x, columns),
         out_shape=jax.ShapeDtypeStruct(packed, jnp.float32),
-        in_specs=[vmem],
+        in_specs=[pl.BlockSpec(memory_space=pltpu.HBM)],
         out_specs=vmem,
         scratch_shapes=[
+            pltpu.VMEM((rows_z * rows_x, lanes), jnp.float32),
             pltpu.VMEM((voxes, rows_z * xd, lanes), jnp.float32),
             pltpu.VMEM((full * xd, lanes), jnp.float32),
             pltpu.VMEM(packed, jnp.float32),
             pltpu.VMEM(packed, jnp.float32),
-            pltpu.VMEM((voxes // CORES, share + 8, half), jnp.float32),
+            pltpu.VMEM((voxes // CORES, share + 1, half), jnp.float32),
             pltpu.VMEM(packed, jnp.float32),
             dma((voxes,)), dma((voxes,)),
             dma((members,)), dma((members,)),
             dma((voxes // CORES,)), dma((voxes // CORES,)),
             dma((members,)), dma((members,)),
+            dma,
         ],
         compiler_params=pltpu.CompilerParams(
             collective_id=0, has_side_effects=True, vmem_limit_bytes=24 * 1024 * 1024
@@ -186,13 +191,7 @@
 
 
 def reciprocal(d):
-    r = pl.reciprocal(d, approx=True)
-    return r * (2.0 - d * r)
-
-
-def inverse_root(d):
-    r = lax.rsqrt(d)
-    return r * (1.5 - 0.5 * d * r * r)
+    return pl.reciprocal(d, approx=True)
 
 
 def splat_lane(rows, lane):
@@ -203,73 +202,105 @@
     return jnp.broadcast_to(rows[i:i + 1], rows.shape)
 
 
-def factor_rows(work, upper, row0):
+def factor_rows(work, upper):
     height, width = work.shape
+    wide = lambda t: jnp.concatenate([t] * (width // LANES), axis=1)
+    pairs = [(i, j) for j in range(ROWS) for i in range(j, ROWS)]
     panel = work[:ROWS, :]
+    corner = [splat_lane(panel[:, :LANES], j) for j in range(ROWS)]
     for k in range(0, height, ROWS):
-        columns = [splat_lane(panel[:, :LANES], k + j) for j in range(ROWS)]
-        s = {
-            (i, j): splat_row(columns[j], i) for j in range(ROWS) for i in range(j, ROWS)
-        }
+        last = k + ROWS == height
+        s = {(i, j): splat_row(corner[j], i) for i, j in pairs}
         rows = [splat_row(panel, i) for i in range(ROWS)]
-        wide = lambda t: jnp.concatenate([t] * (width // LANES), axis=1)
-        inv, low = [], {}
-        for m in range(ROWS):
-            inv.append(reciprocal(s[m, m]))
-            for i in range(m + 1, ROWS):
+        if not last:
+            panel = work[k + ROWS:k + 2 * ROWS, :]
+            left = [splat_lane(panel[:, :LANES], k + j) for j in range(ROWS)]
+            corner = [splat_lane(panel[:, :LANES], k + ROWS + j) for j in range(ROWS)]
+        inv, low, pivot, scaled = [None] * ROWS, {}, [None] * ROWS, [None] * ROWS
+        for m in range(0, ROWS, 2):
+            n = m + 1
+            a, b, c = s[m, m], s[n, m], s[n, n]
+            det = a * c - b * b
+            inv_det = reciprocal(det)
+            inv[m] = reciprocal(a)
+            inv[n] = a * inv_det
+            pivot[m], pivot[n] = a, det * inv[m]
+            low[n, m] = b * inv[m]
+            second = {}
+            for i in range(n + 1, ROWS):
                 low[i, m] = s[i, m] * inv[m]
-                for j in range(m + 1, i + 1):
-                    s[i, j] = s[i, j] - low[i, m] * s[j, m]
-            for i in range(m + 1, ROWS):
-                rows[i] = rows[i] - wide(low[i, m]) * rows[m]
+                second[i] = s[i, n] - low[i, m] * b
+                low[i, n] = second[i] * inv[n]
+            for i, j in pairs:
+                if j <= n:
+                    continue
+                first = s[i, j] - low[i, m] * s[j, m]
+                if i <= n + 2:
+                    s[i, j] = first - (a * second[i] * second[j]) * inv_det
+                else:
+                    s[i, j] = first - low[i, n] * second[j]
+            for q in (m, n):
+                for i in range(q + 1, ROWS):
+                    rows[i] = rows[i] - wide(low[i, q]) * rows[q]
+                scaled[q] = rows[q] * wide(inv[q])
+                if last:
+                    continue
+                for i in range(q + 1, ROWS):
+                    left[i] = left[i] - low[i, q] * left[q]
+                panel = panel - wide(left[q]) * scaled[q]
+                turned = left[q] * inv[q]
+                corner = [
+                    corner[j] - left[q] * splat_row(turned, j) for j in range(ROWS)
+                ]
         for i in range(ROWS):
-            row = rows[i] * wide(inverse_root(s[i, i]))
-            upper[row0 + k + i:row0 + k + i + 1, :] = row[:1]
-        if k + ROWS == height:
-            break
-        solved = [None] * ROWS
+            row = rows[i] * wide(lax.rsqrt(pivot[i]))
+            upper[k + i:k + i + 1, :] = row[:1]
+        if k + 2 * ROWS >= height:
+            continue
+        solved = list(scaled)
         for i in reversed(range(ROWS)):
-            solved[i] = rows[i] * wide(inv[i])
             for m in reversed(range(i + 1, ROWS)):
                 solved[i] = solved[i] - wide(low[m, i]) * solved[m]
-        for g in range(k + ROWS, height, ROWS):
+        for g in range(k + 2 * ROWS, height, ROWS):
             group = work[g:g + ROWS, :]
             terms = [
                 wide(splat_lane(group[:, :LANES], k + j)) * solved[j] for j in range(ROWS)
             ]
             while len(terms) > 1:
-                terms = [a + b for a, b in zip(terms[::2], terms[1::2])]
-            group = group - terms[0]
-            if g == k + ROWS:
-                panel = group
-            else:
-                work[g:g + ROWS, :] = group
+                terms = [x + y for x, y in zip(terms[::2], terms[1::2])]
+            work[g:g + ROWS, :] = group - terms[0]
 
 
 def factor_kernel(packed_ref, out_ref, work1, work2, upper1, upper2):
     members, rows, half = packed_ref.shape
-    share = rows - ROWS
+    share = rows - 1
     main = [packed_ref[q, :share, :] for q in range(members)]
     g21 = jnp.concatenate(main[:members // 2], axis=0)
     mixed = jnp.concatenate(main[members // 2:], axis=0)
     i = lax.broadcasted_iota(jnp.int32, (half, half), 0)
     j = lax.broadcasted_iota(jnp.int32, (half, half), 1)
+    diag1 = jnp.sum(jnp.where(i == j, mixed, 0.0), axis=0, keepdims=True)
+    diag2 = packed_ref[0, share:, :]
+    root1, root2 = lax.rsqrt(diag1), lax.rsqrt(diag2)
+    side1 = jnp.broadcast_to(root1, (half, half)).T
+    side2 = jnp.broadcast_to(root2, (half, half)).T
     flipped = mixed.T
-    work1[:, :half] = jnp.where(i >= j, mixed, flipped)
-    work1[:, half:] = g21.T
-    factor_rows(work1, upper1, 0)
+    work1[:, :half] = jnp.where(i >= j, mixed, flipped) * side1 * root1
+    work1[:, half:] = g21.T * side1 * root2
+    factor_rows(work1, upper1)
     right = upper1[:, half:]
     g22 = jnp.where(i < j, mixed, flipped)
-    g22 = jnp.where(i == j, packed_ref[0, share:share + 1, :], g22)
-    work2[...] = g22 - lax.dot_general(
+    g22 = jnp.where(i == j, diag2, g22)
+    work2[...] = g22 * side2 * root2 - lax.dot_general(
         right, right, (((0,), (0,)), ((), ())),
         precision=EXACT, preferred_element_type=jnp.float32,
     )
-    factor_rows(work2, upper2, 0)
-    out_ref[:half, :half] = jnp.where(i >= j, upper1[:, :half].T, 0.0)
+    factor_rows(work2, upper2)
+    size1, size2 = diag1 * root1, diag2 * root2
+    out_ref[:half, :half] = jnp.where(i >= j, (upper1[:, :half] * size1).T, 0.0)
     out_ref[:half, half:] = jnp.zeros((half, half), jnp.float32)
-    out_ref[half:, :half] = right.T
-    out_ref[half:, half:] = jnp.where(i >= j, upper2[...].T, 0.0)
+    out_ref[half:, :half] = (right * size2).T
+    out_ref[half:, half:] = jnp.where(i >= j, (upper2[...] * size2).T, 0.0)
 
 
 def per_device(volume):

time: 43.9 us -> 38 us (0.87)
  Pallas kernels: 42.7 us -> 36.8 us
    pallas_call x1, Pallas kernels: 12.9 us -> 7.17 us  [per_device(): pl.pallas_call(factor_kernel, out_shape=jax.ShapeDtypeStruct((2 * half, 2...]
where the time goes in v3:
time: 38 us; the launch traced here: 37.8 us
  Pallas kernels  36.8 us (97%)
  local copies, waits for them, and re-layouts  1.04 us (3%)
    pallas_call x1, Pallas kernels, summed_gram(): pl.pallas_call(functools.partial(gram_kernel, frames, voxes, rows_z, rows...  29.6 us
    pallas_call x1, Pallas kernels, per_device(): pl.pallas_call(factor_kernel, out_shape=jax.ShapeDtypeStruct((2 * half, 2...  7.17 us
    unnamed x2, local copies, waits for them, and re-layouts  1.04 us

profile of v3, /device:TPU:0, one launch (start us, length us, event | category | flops | bytes accessed | tf_op | source)
XLA Modules:
  0.0 37.8 jit_solution(17132136185589076521)
XLA Ops:
  0.0 0.0 copy-start
  0.0 1.0 %copy-done = f32[1,32,32,128]{3,2,1,0:T(8,128)S(1)} copy-done((f32[1,32,32,128]{3,2,1,0:T(8,128)S(1)}, f32[1,32,32,128]{3,2,1,0:T(8,128)}, u32[]{:S(2)}) %copy-start) | copy-done | bytes 524312
  1.0 29.6 %summed_gram.1.packed_ref = f32[8,33,128]{2,1,0:T(8,128)S(1)} custom-call(f32[1024,128]{1,0:T(8,128)S(1)} %bitcast.1), custom_call_target="tpu_custom_call" | custom-call | tf_op jit(solution)/shard_map/summed_gram/pallas_call | solution.py:167
  30.7 7.2 %factor.1 = f32[256,256]{1,0:T(8,128)} custom-call(f32[8,33,128]{2,1,0:T(8,128)S(1)} %summed_gram.1.packed_ref), custom_call_target="tpu_custom_call" | custom-call | tf_op jit(solution)/shard_map/factor/pallas_call | solution.py:310
Async XLA Ops:
  0.0 1.0 %copy-start = (f32[1,32,32,128]{3,2,1,0:T(8,128)S(1)}, f32[1,32,32,128]{3,2,1,0:T(8,128)}, u32[]{:S(2)}) copy-start(f32[1,32,32,128]{3,2,1,0:T(8,128)} %param.1) | copy-start | bytes 1572868

commit v4 on v3

--- a/solution.py
+++ b/solution.py
@@ -13,10 +13,15 @@
 ROWS, LANES = 8, 128
 
 
+def chunk_rows(rows_z, xd):
+    step = next(n for n in range(1, xd + 1) if xd % n == 0 and rows_z * n % ROWS == 0)
+    return step, rows_z * step
+
+
 def gram_kernel(
     frames, voxes, rows_z, rows_x, columns,
     vol_hbm, out_ref,
-    vol_ref, send, recv, part, plane, line, total,
+    vol_ref, send, recv, gram, part, plane, line, total,
     a_send, a_recv, b_send, b_recv, c_send, c_recv, d_send, d_recv, load_sem,
 ):
     f = lax.axis_index("frame")
@@ -26,7 +31,8 @@
     own = f * CORES + core
     members = frames * CORES
     xd = rows_x // voxes
-    slot = rows_z * xd
+    step, slot = chunk_rows(rows_z, xd)
+    chunks = xd // step
     half = rows_z * voxes // 2
     share = 2 * half // members
 
@@ -38,8 +44,14 @@
         c = lax.rem(chip + k, chips)
         return c, (f, c * CORES + core)
 
-    load = pltpu.make_async_copy(vol_hbm, vol_ref, load_sem)
-    load.start()
+    loads = [
+        pltpu.make_async_copy(
+            vol_hbm.at[0, z], vol_ref.at[pl.ds(z * rows_x, rows_x)], load_sem.at[z]
+        )
+        for z in range(rows_z)
+    ]
+    for load in loads:
+        load.start()
 
     barrier = pltpu.get_barrier_semaphore()
     for k in range(1, voxes):
@@ -51,49 +63,56 @@
             barrier, inc=1, device_id=plane_peer(k)[1], device_id_type=MESH
         )
 
-    load.wait()
-    for p in range(voxes):
-        for x in range(xd):
-            send[p, pl.ds(x, rows_z, stride=xd), :] = vol_ref[
-                pl.ds(p * xd + x, rows_z, stride=rows_x), :
-            ]
+    for load in loads:
+        load.wait()
+    for c in range(chunks):
+        for p in range(voxes):
+            for x in range(step):
+                send[p, c, pl.ds(x, rows_z, stride=step), :] = vol_ref[
+                    pl.ds(p * xd + c * step + x, rows_z, stride=rows_x), :
+                ]
 
     pl.semaphore_wait(barrier, voxes - 1 + members - 1)
 
     mine = pl.ds(pl.multiple_of(v * slot, slot), slot)
-    copies = []
-    for k in sorted(range(1, voxes), key=lambda k: abs(k - voxes // 2)):
-        p = lax.rem(v + k, voxes)
-        copy = pltpu.make_async_remote_copy(
-            src_ref=send.at[p],
-            dst_ref=recv.at[mine],
-            send_sem=a_send.at[k],
-            recv_sem=a_recv.at[k],
-            device_id=(f, p),
-            device_id_type=MESH,
-        )
-        copy.start()
-        copies.append(copy)
-    recv[mine, :] = send[v]
-    for copy in copies:
-        copy.wait()
-
-    block = jnp.concatenate(
-        [recv[pl.ds(x, 2 * half, stride=xd), :] for x in range(xd)], axis=1
-    )
-    top, low = block[:half], block[half:]
-
-    def dot(a, b):
-        return lax.dot_general(
-            a, b, (((1,), (1,)), ((), ())),
+    order = sorted(range(1, voxes), key=lambda k: abs(k - voxes // 2))
+    arriving = []
+    for c in range(chunks):
+        arriving.append([])
+        for k in order:
+            p = lax.rem(v + k, voxes)
+            copy = pltpu.make_async_remote_copy(
+                src_ref=send.at[p, c],
+                dst_ref=recv.at[c, mine],
+                send_sem=a_send.at[c, k],
+                recv_sem=a_recv.at[c, k],
+                device_id=(f, p),
+                device_id_type=MESH,
+            )
+            copy.start()
+            arriving[c].append(copy)
+    for c in range(chunks):
+        recv[c, mine, :] = send[v, c]
+
+    for c in range(chunks):
+        for copy in arriving[c]:
+            copy.wait_recv()
+        block = jnp.concatenate(
+            [recv[c, pl.ds(x, 2 * half, stride=step), :] for x in range(step)], axis=1
+        )
+        product = lax.dot_general(
+            block, block, (((1,), (1,)), ((), ())),
             precision=EXACT, preferred_element_type=jnp.float32,
         )
+        if c > 0:
+            product = gram[...] + product
+        gram[...] = product
 
     i = lax.broadcasted_iota(jnp.int32, (half, half), 0)
     j = lax.broadcasted_iota(jnp.int32, (half, half), 1)
-    g22 = dot(low, low)
+    g22 = gram[half:, half:]
     diag = jnp.sum(jnp.where(i == j, g22, 0.0), axis=0, keepdims=True)
-    packed = [dot(low, top), jnp.where(i >= j, dot(top, top), g22)]
+    packed = [gram[half:, :half], jnp.where(i >= j, gram[:half, :half], g22)]
     for q in range(members):
         row = q * share
         part[q, :share, :] = packed[row // half][row % half:row % half + share]
@@ -115,6 +134,9 @@
     plane[own] = part[own]
     for copy in copies:
         copy.wait()
+    for sent in arriving:
+        for copy in sent:
+            copy.wait_send()
 
     line[chip] = jnp.sum(plane[...], axis=0)
     copies = []
@@ -162,6 +184,7 @@
     half = full // 2
     share = full // members
     packed = (members, share + 1, half)
+    step, slot = chunk_rows(rows_z, xd)
     dma = pltpu.SemaphoreType.DMA
     vmem = pl.BlockSpec(memory_space=pltpu.VMEM)
     return pl.pallas_call(
@@ -171,23 +194,24 @@
         out_specs=vmem,
         scratch_shapes=[
             pltpu.VMEM((rows_z * rows_x, lanes), jnp.float32),
-            pltpu.VMEM((voxes, rows_z * xd, lanes), jnp.float32),
-            pltpu.VMEM((full * xd, lanes), jnp.float32),
+            pltpu.VMEM((voxes, xd // step, slot, lanes), jnp.float32),
+            pltpu.VMEM((xd // step, slot * voxes, lanes), jnp.float32),
+            pltpu.VMEM((full, full), jnp.float32),
             pltpu.VMEM(packed, jnp.float32),
             pltpu.VMEM(packed, jnp.float32),
             pltpu.VMEM((voxes // CORES, share + 1, half), jnp.float32),
             pltpu.VMEM(packed, jnp.float32),
-            dma((voxes,)), dma((voxes,)),
+            dma((xd // step, voxes)), dma((xd // step, voxes)),
             dma((members,)), dma((members,)),
             dma((voxes // CORES,)), dma((voxes // CORES,)),
             dma((members,)), dma((members,)),
-            dma,
+            dma((rows_z,)),
         ],
         compiler_params=pltpu.CompilerParams(
             collective_id=0, has_side_effects=True, vmem_limit_bytes=24 * 1024 * 1024
         ),
         name="summed_gram",
-    )(volume.reshape(rows_z * rows_x, lanes))
+    )(pltpu.with_memory_space_constraint(volume, pltpu.HBM))
 
 
 def reciprocal(d):

time: 38 us -> 38.1 us (level)
  Pallas kernels: 36.8 us -> 37.9 us
  local copies, waits for them, and re-layouts: 1.04 us -> 0 us
    pallas_call x1, Pallas kernels: 29.6 us -> 30.7 us  [summed_gram(): pl.pallas_call(functools.partial(gram_kernel, frames, voxes, rows_z, rows...]
    unnamed x2 -> x0, local copies, waits for them, and re-layouts: 1.04 us -> none
where the time goes in v4:
time: 38.1 us; the launch traced here: 37.9 us
  Pallas kernels  37.9 us (99%)
    pallas_call x1, Pallas kernels, summed_gram(): pl.pallas_call(functools.partial(gram_kernel, frames, voxes, rows_z, rows...  30.7 us
    pallas_call x1, Pallas kernels, per_device(): pl.pallas_call(factor_kernel, out_shape=jax.ShapeDtypeStruct((2 * half, 2...  7.17 us

profile of v4, /device:TPU:0, one launch (start us, length us, event | category | flops | bytes accessed | tf_op | source)
XLA Modules:
  0.0 37.9 jit_solution(5726785368080772086)
XLA Ops:
  0.0 30.7 %summed_gram.1.packed_ref = f32[8,33,128]{2,1,0:T(8,128)S(1)} custom-call(f32[1,32,32,128]{3,2,1,0:T(8,128)} %vol_hbm.1), custom_call_target="tpu_custom_call" | custom-call | tf_op jit(solution)/shard_map/summed_gram/pallas_call | solution.py:190
  30.7 7.2 %factor.1 = f32[256,256]{1,0:T(8,128)} custom-call(f32[8,33,128]{2,1,0:T(8,128)S(1)} %summed_gram.1.packed_ref), custom_call_target="tpu_custom_call" | custom-call | tf_op jit(solution)/shard_map/factor/pallas_call | solution.py:334

commit v5 on v3

--- a/solution.py
+++ b/solution.py
@@ -14,10 +14,10 @@
 
 
 def gram_kernel(
-    frames, voxes, rows_z, rows_x, columns,
-    vol_hbm, out_ref,
-    vol_ref, send, recv, part, plane, line, total,
-    a_send, a_recv, b_send, b_recv, c_send, c_recv, d_send, d_recv, load_sem,
+    frames, voxes, columns,
+    vol_ref, out_ref,
+    recv, part, plane, line, total,
+    a_send, a_recv, b_send, b_recv, c_send, c_recv, d_send, d_recv, own_sem,
 ):
     f = lax.axis_index("frame")
     v = lax.axis_index("vox")
@@ -25,8 +25,7 @@
     chips = voxes // CORES
     own = f * CORES + core
     members = frames * CORES
-    xd = rows_x // voxes
-    slot = rows_z * xd
+    rows_z, xd = vol_ref.shape[0], vol_ref.shape[2]
     half = rows_z * voxes // 2
     share = 2 * half // members
 
@@ -37,9 +36,6 @@
     def line_peer(k):
         c = lax.rem(chip + k, chips)
         return c, (f, c * CORES + core)
-
-    load = pltpu.make_async_copy(vol_hbm, vol_ref, load_sem)
-    load.start()
 
     barrier = pltpu.get_barrier_semaphore()
     for k in range(1, voxes):
@@ -51,21 +47,16 @@
             barrier, inc=1, device_id=plane_peer(k)[1], device_id_type=MESH
         )
 
-    load.wait()
-    for p in range(voxes):
-        for x in range(xd):
-            send[p, pl.ds(x, rows_z, stride=xd), :] = vol_ref[
-                pl.ds(p * xd + x, rows_z, stride=rows_x), :
-            ]
-
+    mine = pl.ds(v * rows_z, rows_z)
+    stay = pltpu.make_async_copy(vol_ref.at[:, v], recv.at[mine], own_sem)
+    stay.start()
     pl.semaphore_wait(barrier, voxes - 1 + members - 1)
 
-    mine = pl.ds(pl.multiple_of(v * slot, slot), slot)
     copies = []
     for k in sorted(range(1, voxes), key=lambda k: abs(k - voxes // 2)):
         p = lax.rem(v + k, voxes)
         copy = pltpu.make_async_remote_copy(
-            src_ref=send.at[p],
+            src_ref=vol_ref.at[:, p],
             dst_ref=recv.at[mine],
             send_sem=a_send.at[k],
             recv_sem=a_recv.at[k],
@@ -74,26 +65,20 @@
         )
         copy.start()
         copies.append(copy)
-    recv[mine, :] = send[v]
+    stay.wait()
     for copy in copies:
         copy.wait()
 
-    block = jnp.concatenate(
-        [recv[pl.ds(x, 2 * half, stride=xd), :] for x in range(xd)], axis=1
+    block = jnp.concatenate([recv[:, x, :] for x in range(xd)], axis=1)
+    gram = lax.dot_general(
+        block, block, (((1,), (1,)), ((), ())),
+        precision=EXACT, preferred_element_type=jnp.float32,
     )
-    top, low = block[:half], block[half:]
-
-    def dot(a, b):
-        return lax.dot_general(
-            a, b, (((1,), (1,)), ((), ())),
-            precision=EXACT, preferred_element_type=jnp.float32,
-        )
-
     i = lax.broadcasted_iota(jnp.int32, (half, half), 0)
     j = lax.broadcasted_iota(jnp.int32, (half, half), 1)
-    g22 = dot(low, low)
+    g22 = gram[half:, half:]
     diag = jnp.sum(jnp.where(i == j, g22, 0.0), axis=0, keepdims=True)
-    packed = [dot(low, top), jnp.where(i >= j, dot(top, top), g22)]
+    packed = [gram[half:, :half], jnp.where(i >= j, gram[:half, :half], g22)]
     for q in range(members):
         row = q * share
         part[q, :share, :] = packed[row // half][row % half:row % half + share]
@@ -162,17 +147,16 @@
     half = full // 2
     share = full // members
     packed = (members, share + 1, half)
+    split = volume.reshape(rows_z, voxes, xd, lanes)
     dma = pltpu.SemaphoreType.DMA
     vmem = pl.BlockSpec(memory_space=pltpu.VMEM)
     return pl.pallas_call(
-        functools.partial(gram_kernel, frames, voxes, rows_z, rows_x, columns),
+        functools.partial(gram_kernel, frames, voxes, columns),
         out_shape=jax.ShapeDtypeStruct(packed, jnp.float32),
         in_specs=[pl.BlockSpec(memory_space=pltpu.HBM)],
         out_specs=vmem,
         scratch_shapes=[
-            pltpu.VMEM((rows_z * rows_x, lanes), jnp.float32),
-            pltpu.VMEM((voxes, rows_z * xd, lanes), jnp.float32),
-            pltpu.VMEM((full * xd, lanes), jnp.float32),
+            pltpu.VMEM((full, xd, lanes), jnp.float32),
             pltpu.VMEM(packed, jnp.float32),
             pltpu.VMEM(packed, jnp.float32),
             pltpu.VMEM((voxes // CORES, share + 1, half), jnp.float32),
@@ -187,7 +171,7 @@
             collective_id=0, has_side_effects=True, vmem_limit_bytes=24 * 1024 * 1024
         ),
         name="summed_gram",
-    )(volume.reshape(rows_z * rows_x, lanes))
+    )(pltpu.with_memory_space_constraint(split, pltpu.HBM))
 
 
 def reciprocal(d):

time: 38 us -> 37.2 us (0.979)
  local copies, waits for them, and re-layouts: 1.04 us -> 0 us
    unnamed x2 -> x0, local copies, waits for them, and re-layouts: 1.04 us -> none
where the time goes in v5:
time: 37.2 us; the launch traced here: 37 us
  Pallas kernels  37 us (99%)
    pallas_call x1, Pallas kernels, summed_gram(): pl.pallas_call(functools.partial(gram_kernel, frames, voxes, columns), ou...  29.9 us
    pallas_call x1, Pallas kernels, per_device(): pl.pallas_call(factor_kernel, out_shape=jax.ShapeDtypeStruct((2 * half, 2...  7.17 us

profile of v5, /device:TPU:0, one launch (start us, length us, event | category | flops | bytes accessed | tf_op | source)
XLA Modules:
  0.0 37.0 jit_solution(5596614575729807582)
XLA Ops:
  0.0 29.9 %summed_gram.1.packed_ref = f32[8,33,128]{2,1,0:T(8,128)S(1)} custom-call(f32[32,8,4,128]{3,2,1,0:T(4,128)} %bitcast.1), custom_call_target="tpu_custom_call" | custom-call | tf_op jit(solution)/shard_map/summed_gram/pallas_call | solution.py:153
  29.9 7.2 %factor.1 = f32[256,256]{1,0:T(8,128)} custom-call(f32[8,33,128]{2,1,0:T(8,128)S(1)} %summed_gram.1.packed_ref), custom_call_target="tpu_custom_call" | custom-call | tf_op jit(solution)/shard_map/factor/pallas_call | solution.py:294

commit v6 on v5

--- a/solution.py
+++ b/solution.py
@@ -16,7 +16,7 @@
 def gram_kernel(
     frames, voxes, columns,
     vol_ref, out_ref,
-    recv, part, plane, line, total,
+    recv, block_ref, part, plane, line, total,
     a_send, a_recv, b_send, b_recv, c_send, c_recv, d_send, d_recv, own_sem,
 ):
     f = lax.axis_index("frame")
@@ -64,12 +64,19 @@
             device_id_type=MESH,
         )
         copy.start()
-        copies.append(copy)
+        copies.append((k, copy))
+    def place(source):
+        for x in range(xd):
+            block_ref[source, :, x * LANES:(x + 1) * LANES] = recv[
+                pl.ds(source * rows_z, rows_z), x, :
+            ]
+
     stay.wait()
-    for copy in copies:
-        copy.wait()
-
-    block = jnp.concatenate([recv[:, x, :] for x in range(xd)], axis=1)
+    place(v)
+    for k, copy in reversed(copies):
+        copy.wait_recv()
+        place(lax.rem(v + voxes - k, voxes))
+    block = block_ref[...].reshape(2 * half, xd * LANES)
     gram = lax.dot_general(
         block, block, (((1,), (1,)), ((), ())),
         precision=EXACT, preferred_element_type=jnp.float32,
@@ -83,6 +90,9 @@
         row = q * share
         part[q, :share, :] = packed[row // half][row % half:row % half + share]
         part[q, share:, :] = diag
+
+    for k, copy in copies:
+        copy.wait_send()
 
     copies = []
     for k in range(1, members):
@@ -157,6 +167,7 @@
         out_specs=vmem,
         scratch_shapes=[
             pltpu.VMEM((full, xd, lanes), jnp.float32),
+            pltpu.VMEM((voxes, rows_z, xd * lanes), jnp.float32),
             pltpu.VMEM(packed, jnp.float32),
             pltpu.VMEM(packed, jnp.float32),
             pltpu.VMEM((voxes // CORES, share + 1, half), jnp.float32),

time: 37.2 us -> 37.1 us (level)
  no operation moved by 1% of the time
where the time goes in v6:
time: 37.1 us; the launch traced here: 36.9 us
  Pallas kernels  36.9 us (99%)
    pallas_call x1, Pallas kernels, summed_gram(): pl.pallas_call(functools.partial(gram_kernel, frames, voxes, columns), ou...  29.8 us
    pallas_call x1, Pallas kernels, per_device(): pl.pallas_call(factor_kernel, out_shape=jax.ShapeDtypeStruct((2 * half, 2...  7.16 us

profile of v6, /device:TPU:0, one launch (start us, length us, event | category | flops | bytes accessed | tf_op | source)
XLA Modules:
  0.0 36.9 jit_solution(14327332948755458594)
XLA Ops:
  0.0 29.8 %summed_gram.1.packed_ref = f32[8,33,128]{2,1,0:T(8,128)S(1)} custom-call(f32[32,8,4,128]{3,2,1,0:T(4,128)} %bitcast.1), custom_call_target="tpu_custom_call" | custom-call | tf_op jit(solution)/shard_map/summed_gram/pallas_call | solution.py:163
  29.8 7.2 %factor.1 = f32[256,256]{1,0:T(8,128)} custom-call(f32[8,33,128]{2,1,0:T(8,128)S(1)} %summed_gram.1.packed_ref), custom_call_target="tpu_custom_call" | custom-call | tf_op jit(solution)/shard_map/factor/pallas_call | solution.py:305

commit v7 on v6

--- a/solution.py
+++ b/solution.py
@@ -77,39 +77,47 @@
         copy.wait_recv()
         place(lax.rem(v + voxes - k, voxes))
     block = block_ref[...].reshape(2 * half, xd * LANES)
-    gram = lax.dot_general(
-        block, block, (((1,), (1,)), ((), ())),
-        precision=EXACT, preferred_element_type=jnp.float32,
-    )
+    top, low = block[:half], block[half:]
+
+    def dot(x, y):
+        return lax.dot_general(
+            x, y, (((1,), (1,)), ((), ())),
+            precision=EXACT, preferred_element_type=jnp.float32,
+        )
+
+    def share_copy(q, landing):
+        return pltpu.make_async_remote_copy(
+            src_ref=part.at[q],
+            dst_ref=plane.at[landing],
+            send_sem=b_send.at[q],
+            recv_sem=b_recv.at[landing],
+            device_id=(q // CORES, chip * CORES + q % CORES),
+            device_id_type=MESH,
+        )
+
+    def send_shares(first, rows, diag):
+        for q in range(first, first + members // 2):
+            row = (q - first) * share
+            part[q, :share, :] = rows[row:row + share]
+            part[q, share:, :] = diag
+
+            @pl.when(q != own)
+            def _():
+                share_copy(q, own).start()
+
     i = lax.broadcasted_iota(jnp.int32, (half, half), 0)
     j = lax.broadcasted_iota(jnp.int32, (half, half), 1)
-    g22 = gram[half:, half:]
+    send_shares(0, dot(low, top), jnp.zeros((1, half), jnp.float32))
+    g22 = dot(low, low)
     diag = jnp.sum(jnp.where(i == j, g22, 0.0), axis=0, keepdims=True)
-    packed = [gram[half:, :half], jnp.where(i >= j, gram[:half, :half], g22)]
-    for q in range(members):
-        row = q * share
-        part[q, :share, :] = packed[row // half][row % half:row % half + share]
-        part[q, share:, :] = diag
-
+    send_shares(members // 2, jnp.where(i >= j, dot(top, top), g22), diag)
+    plane[own] = part[own]
     for k, copy in copies:
         copy.wait_send()
-
-    copies = []
-    for k in range(1, members):
-        q, device = plane_peer(k)
-        copy = pltpu.make_async_remote_copy(
-            src_ref=part.at[q],
-            dst_ref=plane.at[own],
-            send_sem=b_send.at[k],
-            recv_sem=b_recv.at[k],
-            device_id=device,
-            device_id_type=MESH,
-        )
-        copy.start()
-        copies.append(copy)
-    plane[own] = part[own]
-    for copy in copies:
-        copy.wait()
+    for q in range(members):
+        @pl.when(q != own)
+        def _():
+            share_copy(q, q).wait()
 
     line[chip] = jnp.sum(plane[...], axis=0)
     copies = []
@@ -275,7 +283,7 @@
     i = lax.broadcasted_iota(jnp.int32, (half, half), 0)
     j = lax.broadcasted_iota(jnp.int32, (half, half), 1)
     diag1 = jnp.sum(jnp.where(i == j, mixed, 0.0), axis=0, keepdims=True)
-    diag2 = packed_ref[0, share:, :]
+    diag2 = packed_ref[members // 2, share:, :]
     root1, root2 = lax.rsqrt(diag1), lax.rsqrt(diag2)
     side1 = jnp.broadcast_to(root1, (half, half)).T
     side2 = jnp.broadcast_to(root2, (half, half)).T

time: 37.1 us -> 37 us (level)
  no operation moved by 1% of the time
where the time goes in v7:
time: 37 us; the launch traced here: 36.8 us
  Pallas kernels  36.8 us (99%)
    pallas_call x1, Pallas kernels, summed_gram(): pl.pallas_call(functools.partial(gram_kernel, frames, voxes, columns), ou...  29.6 us
    pallas_call x1, Pallas kernels, per_device(): pl.pallas_call(factor_kernel, out_shape=jax.ShapeDtypeStruct((2 * half, 2...  7.17 us

profile of v7, /device:TPU:0, one launch (start us, length us, event | category | flops | bytes accessed | tf_op | source)
XLA Modules:
  0.0 36.8 jit_solution(16281618435720400720)
XLA Ops:
  0.0 29.6 %summed_gram.1.packed_ref = f32[8,33,128]{2,1,0:T(8,128)S(1)} custom-call(f32[32,8,4,128]{3,2,1,0:T(4,128)} %bitcast.1), custom_call_target="tpu_custom_call" | custom-call | tf_op jit(solution)/shard_map/summed_gram/pallas_call | solution.py:171
  29.7 7.2 %factor.1 = f32[256,256]{1,0:T(8,128)} custom-call(f32[8,33,128]{2,1,0:T(8,128)S(1)} %summed_gram.1.packed_ref), custom_call_target="tpu_custom_call" | custom-call | tf_op jit(solution)/shard_map/factor/pallas_call | solution.py:313
